TPU v7x, 32 devices: a whole 2x2x4 slice. The times are simulated.
32 devices in a mesh: dp: 4 (over y, core), slab: 8 (over z, x).
Axes of the slice: x: 2, y: 2, z: 4, core: 2. Of those that a mesh axis runs over, the one named last changes fastest.
Arguments:
- u_field: bfloat16 [4, 128, 32, 128, 128], P('dp', 'slab'), may hold values from -6 to 6
- preact: bfloat16 [4, 128, 32, 128, 128], P('dp', 'slab'), may hold values from -6 to 6
- cotangent: bfloat16 [4, 128, 32, 128, 128], P('dp', 'slab'), may hold values from -6 to 6
- weights: bfloat16 [16, 256, 2048], P(None, 'slab'), may hold values from -6 to 6
Outputs:
- grad_weights: float32 [16, 256, 2048], P('dp', 'slab')
- grad_field: bfloat16 [4, 128, 32, 128, 128], P('dp', 'slab')
All inputs are finite; a program needn't handle non-finite values.
Results may differ from a plain program's by a relative error of at most 0.0055.
Values sent between devices are 32-bit elements; how exact they have to be, the bound alone decides.
A program may use at most 192 MiB of HBM per device.

v0:
```python
import math

import jax
import jax.numpy as jnp
from jax import lax
from jax.sharding import PartitionSpec as P

C = 32
NX = 128
NY = 128
NZ = 128
MX = 16
MY = 16
MZ = 16


exact_mode = lax.Precision.HIGHEST


def signed_freqs(count):
    index = jnp.arange(count, dtype=jnp.int32)
    return jnp.where(index < count // 2, index, index - count)


def twiddles(length, freqs):
    product = jnp.arange(length, dtype=jnp.int32)[:, None] * freqs[None, :] % length
    angle = product.astype(jnp.float32) * (2.0 * math.pi / length)
    return (jnp.cos(angle), jnp.sin(angle))


def gelu_slope(pre):
    return 0.5 * (1.0 + lax.erf(pre * (1.0 / math.sqrt(2.0)))) + pre * jnp.exp(-0.5 * pre * pre) * (
        1.0 / math.sqrt(2.0 * math.pi)
    )


def transform_planes(field, zcos_low, zsin_low, cos_y, sin_y):
    plane_real = jnp.einsum("xcyz,zk->xcyk", field, zcos_low, preferred_element_type=jnp.float32)
    plane_imag = jnp.einsum("xcyz,zk->xcyk", field, zsin_low, preferred_element_type=jnp.float32)
    out_real = jnp.einsum("xcyk,ym->mkxc", plane_real, cos_y, precision=exact_mode) + jnp.einsum(
        "xcyk,ym->mkxc", plane_imag, sin_y, precision=exact_mode
    )
    out_imag = jnp.einsum("xcyk,ym->mkxc", plane_imag, cos_y, precision=exact_mode) - jnp.einsum(
        "xcyk,ym->mkxc", plane_real, sin_y, precision=exact_mode
    )
    return (out_real, out_imag)


def body(u_field, preact, cotangent, weights):
    planes = u_field.shape[1]
    slab_count = lax.axis_size("slab")
    slab_index = lax.axis_index("slab")
    owned_rows = MY * MZ // slab_count
    cos_x, sin_x = twiddles(NX, signed_freqs(MX))
    cos_y, sin_y = twiddles(NY, signed_freqs(MY))
    cos_z, sin_z = twiddles(NZ, jnp.arange(MZ, dtype=jnp.int32))
    zcos_low = cos_z.astype(jnp.bfloat16)
    zsin_low = (-sin_z).astype(jnp.bfloat16)
    mode_scale = (jnp.where(jnp.arange(MZ) == 0, 1.0, 2.0) / (NX * NY * NZ)).astype(jnp.float32)
    slope = gelu_slope(preact[0].astype(jnp.float32))
    grad_out = (cotangent[0].astype(jnp.float32) * slope).astype(jnp.bfloat16)
    ub_real, ub_imag = transform_planes(u_field[0], zcos_low, zsin_low, cos_y, sin_y)
    gb_real, gb_imag = transform_planes(grad_out, zcos_low, zsin_low, cos_y, sin_y)
    gb_real = gb_real * mode_scale[None, :, None, None]
    gb_imag = gb_imag * mode_scale[None, :, None, None]
    partial_value = jnp.stack([ub_real, ub_imag, gb_real, gb_imag], axis=3).reshape(
        MY * MZ, planes, 4 * C
    )
    start = slab_index * planes
    count = partial_value.shape[1]
    cos_part = lax.dynamic_slice_in_dim(cos_x, start, count, 0)
    sin_part = lax.dynamic_slice_in_dim(sin_x, start, count, 0)
    split = partial_value.reshape(partial_value.shape[0], count, 2, 2, C)
    part_real = split[:, :, :, 0]
    part_imag = split[:, :, :, 1]
    out_real = jnp.einsum("nxfc,xm->nmfc", part_real, cos_part, precision=exact_mode) + jnp.einsum(
        "nxfc,xm->nmfc", part_imag, sin_part, precision=exact_mode
    )
    out_imag = jnp.einsum("nxfc,xm->nmfc", part_imag, cos_part, precision=exact_mode) - jnp.einsum(
        "nxfc,xm->nmfc", part_real, sin_part, precision=exact_mode
    )
    owned = lax.psum_scatter(
        jnp.stack([out_real, out_imag], axis=3).reshape(partial_value.shape[0], MX, 4 * C),
        "slab",
        scatter_dimension=0,
        tiled=True,
    )
    owned_split = owned.reshape(owned_rows, MX, 2, 2, C)
    g_real = owned_split[:, :, 1, 0]
    g_imag = owned_split[:, :, 1, 1]
    split_weights = weights.astype(jnp.float32).reshape(MX, owned_rows, 2, C, C)
    weight_real = split_weights[:, :, 0]
    weight_imag = split_weights[:, :, 1]
    back_real = jnp.einsum("mkio,kmo->kmi", weight_real, g_real, precision=exact_mode) + jnp.einsum(
        "mkio,kmo->kmi", weight_imag, g_imag, precision=exact_mode
    )
    back_imag = jnp.einsum("mkio,kmo->kmi", weight_real, g_imag, precision=exact_mode) - jnp.einsum(
        "mkio,kmo->kmi", weight_imag, g_real, precision=exact_mode
    )
    swapped = lax.all_to_all(owned[:, :, None, :], "dp", split_axis=1, concat_axis=2, tiled=True)
    mode_share = swapped.shape[1]
    swap_split = swapped.reshape(owned_rows, mode_share, swapped.shape[2], 2, 2, C)
    su_real = swap_split[:, :, :, 0, 0]
    su_imag = swap_split[:, :, :, 0, 1]
    sg_real = swap_split[:, :, :, 1, 0]
    sg_imag = swap_split[:, :, :, 1, 1]
    grad_real = jnp.einsum("kmsi,kmso->mkio", su_real, sg_real, precision=exact_mode) + jnp.einsum(
        "kmsi,kmso->mkio", su_imag, sg_imag, precision=exact_mode
    )
    grad_imag = jnp.einsum("kmsi,kmso->mkio", su_real, sg_imag, precision=exact_mode) - jnp.einsum(
        "kmsi,kmso->mkio", su_imag, sg_real, precision=exact_mode
    )
    grad_weights = jnp.stack([grad_real, grad_imag], axis=2).reshape(
        mode_share, owned_rows, 2 * C * C
    )
    back = jnp.stack([back_real, back_imag], axis=2).reshape(owned_rows, MX, 2 * C)
    block = lax.all_gather(back, "slab", axis=0, tiled=True)
    start = slab_index * planes
    cos_part = lax.dynamic_slice_in_dim(cos_x, start, planes, 0)
    sin_part = lax.dynamic_slice_in_dim(sin_x, start, planes, 0)
    split = block.reshape(block.shape[0], MX, 2, C)
    part_real = split[:, :, 0]
    part_imag = split[:, :, 1]
    rows_real = jnp.einsum("nmc,xm->nxc", part_real, cos_part, precision=exact_mode) - jnp.einsum(
        "nmc,xm->nxc", part_imag, sin_part, precision=exact_mode
    )
    rows_imag = jnp.einsum("nmc,xm->nxc", part_imag, cos_part, precision=exact_mode) + jnp.einsum(
        "nmc,xm->nxc", part_real, sin_part, precision=exact_mode
    )
    spread = jnp.stack([rows_real, rows_imag], axis=2).reshape(block.shape[0], planes, 2 * C)
    spread_split = spread.reshape(MY, MZ, planes, 2, C)
    rows_real = spread_split[:, :, :, 0]
    rows_imag = spread_split[:, :, :, 1]
    plane_real = jnp.einsum("mkxc,ym->xcyk", rows_real, cos_y, precision=exact_mode) - jnp.einsum(
        "mkxc,ym->xcyk", rows_imag, sin_y, precision=exact_mode
    )
    plane_imag = jnp.einsum("mkxc,ym->xcyk", rows_imag, cos_y, precision=exact_mode) + jnp.einsum(
        "mkxc,ym->xcyk", rows_real, sin_y, precision=exact_mode
    )
    field_grad = jnp.einsum("xcyk,zk->xcyz", plane_real, cos_z, precision=exact_mode) - jnp.einsum(
        "xcyk,zk->xcyz", plane_imag, sin_z, precision=exact_mode
    )
    return (grad_weights, field_grad.astype(jnp.bfloat16)[None])


def solution(mesh):
    placed = (
        P("dp", "slab", None, None, None),
        P("dp", "slab", None, None, None),
        P("dp", "slab", None, None, None),
        P(None, "slab", None),
    )
    return jax.shard_map(
        body,
        mesh=mesh,
        in_specs=placed,
        out_specs=(P("dp", "slab", None), P("dp", "slab", None, None, None)),
        check_vma=False,
    )
```

profile of v0, /device:TPU:0, one launch (start us, length us, event | category | flops | bytes accessed | tf_op | source)
XLA Modules:
  0.0 536.0 jit_solution(14479169823925412940)
XLA Ops:
  7.2 18.2 %fusion.7 = bf16[16,32,128,128]{3,2,1,0:T(8,128)(2,1)S(1)} fusion(bf16[1,16,32,128,128]{4,3,2,1,0:T(8,128)(2,1)} %param.6, bf16[1,16,32,128,128]{4,3,2,1,0:T(8,128)(2,1)} %param.5), kind=kLoop, calls=%fused_computation.12 | loop fusion | flops 100663296 | bytes 50331648 | tf_op jit(solution)/shard_map/convert_element_type | solution.py:61
  25.4 4.5 fusion.127
  29.9 6.1 %fusion.117 = f32[16,32,128,16]{2,3,1,0:T(8,128)} fusion(bf16[16,32,128,128]{3,2,1,0:T(8,128)(2,1)S(1)} %fusion.7), kind=kOutput, calls=%fused_computation.142 | convolution fusion | flops 268466176 | bytes 20971520 | tf_op jit(solution)/shard_map/xcyz,zk->xcyk/dot_general | solution.py:38
  36.1 17.8 %fusion.20 = f32[16,16,32,16]{2,0,3,1:T(8,128)} fusion(f32[16,32,128,16]{2,3,1,0:T(8,128)S(1)} %fusion.127, s32[16]{0:T(128)S(1)} %compare_select_fusion), kind=kOutput, calls=%fused_computation.29 | convolution fusion | flops 201355264 | bytes 4718656 | tf_op jit(solution)/shard_map/xcyk,ym->mkxc/dot_general | solution.py:40
  53.8 16.6 %fusion.18 = f32[16,16,32,16]{2,0,3,1:T(8,128)S(1)} fusion(f32[16,32,128,16]{2,3,1,0:T(8,128)S(1)} %fusion.127, s32[16]{0:T(128)S(1)} %compare_select_fusion), kind=kOutput, calls=%fused_computation.27 | convolution fusion | flops 201355264 | bytes 4718656 | tf_op jit(solution)/shard_map/xcyk,ym->mkxc/dot_general | solution.py:43
  70.4 12.3 %fusion.45 = f32[16,32,128,16]{2,3,1,0:T(8,128)} fusion(bf16[1,16,32,128,128]{4,3,2,1,0:T(8,128)(2,1)} %param.4), kind=kOutput, calls=%fused_computation.52 | convolution fusion | flops 268468224 | bytes 20971520 | tf_op jit(solution)/shard_map/xcyz,zk->xcyk/dot_general | solution.py:39
  82.7 12.2 %fusion.42 = f32[16,32,128,16]{2,3,1,0:T(8,128)} fusion(bf16[1,16,32,128,128]{4,3,2,1,0:T(8,128)(2,1)} %param.4), kind=kOutput, calls=%fused_computation.51 | convolution fusion | flops 268466176 | bytes 20971520 | tf_op jit(solution)/shard_map/xcyz,zk->xcyk/dot_general | solution.py:38
  94.9 18.7 %fusion.28 = f32[16,16,32,16]{2,0,3,1:T(8,128)S(1)} fusion(f32[16,32,128,16]{2,3,1,0:T(8,128)} %fusion.45, s32[16]{0:T(128)S(1)} %compare_select_fusion), kind=kOutput, calls=%fused_computation.37 | convolution fusion | flops 201355264 | bytes 4718656 | tf_op jit(solution)/shard_map/xcyk,ym->mkxc/dot_general | solution.py:40
  113.6 16.4 %fusion.26 = f32[16,16,32,16]{2,0,3,1:T(8,128)S(1)} fusion(f32[16,32,128,16]{2,3,1,0:T(8,128)S(1)} %copy-done.2, s32[16]{0:T(128)S(1)} %compare_select_fusion), kind=kOutput, calls=%fused_computation.35 | convolution fusion | flops 201355264 | bytes 4718656 | tf_op jit(solution)/shard_map/xcyk,ym->mkxc/dot_general | solution.py:43
  130.2 16.6 %multiply_bitcast_fusion.1 = f32[16,16,16,1,32]{4,0,1,2,3:T(8,128)S(1)} fusion(f32[16,16,32,16]{2,0,3,1:T(8,128)S(1)} %copy-done.7, f32[16,32,128,16]{2,3,1,0:T(8,128)S(1)} %copy-done, f32[16]{0:T(128)S(1)} %fusion.144, s32[16]{0:T(128)S(1)} %compare_select_fusion), kind=kOutput, calls=%fused_computation.57 | convolution fusion | flops 201617408 | bytes 5243008 | tf_op jit(solution)/shard_map/xcyk,ym->mkxc/dot_general | solution.py:40
  146.8 16.6 %multiply_bitcast_fusion = f32[16,16,16,1,32]{4,0,1,2,3:T(8,128)S(1)} fusion(f32[16,16,32,16]{2,0,3,1:T(8,128)S(1)} %fusion.18, f32[16,32,128,16]{2,3,1,0:T(8,128)S(1)} %copy-done, f32[16]{0:T(128)S(1)} %fusion.144, s32[16]{0:T(128)S(1)} %compare_select_fusion), kind=kOutput, calls=%fused_computation.56 | convolution fusion | flops 201617408 | bytes 5243008 | tf_op jit(solution)/shard_map/xcyk,ym->mkxc/dot_general | solution.py:43
  163.4 16.4 %add_bitcast_fusion.1 = f32[16,16,16,1,32]{4,0,1,2,3:T(8,128)S(1)} fusion(f32[16,16,32,16]{2,0,3,1:T(8,128)S(1)} %fusion.28, f32[16,32,128,16]{2,3,1,0:T(8,128)S(1)} %copy-done.1, s32[16]{0:T(128)S(1)} %compare_select_fusion), kind=kOutput, calls=%fused_computation.59 | convolution fusion | flops 201486336 | bytes 5242944 | tf_op jit(solution)/shard_map/xcyk,ym->mkxc/dot_general | solution.py:40
  179.8 16.8 %subtract_bitcast_fusion.1 = f32[16,16,16,1,32]{4,0,1,2,3:T(8,128)S(1)} fusion(f32[16,16,32,16]{2,0,3,1:T(8,128)S(1)} %fusion.26, f32[16,32,128,16]{2,3,1,0:T(8,128)S(1)} %copy-done.1, s32[16]{0:T(128)S(1)} %compare_select_fusion), kind=kOutput, calls=%fused_computation.58 | convolution fusion | flops 201486336 | bytes 5242944 | tf_op jit(solution)/shard_map/xcyk,ym->mkxc/dot_general | solution.py:43
  197.2 4.9 copy.50
  202.0 4.4 fusion.225
  206.5 4.1 copy.97
  210.5 4.2 copy.98
  219.2 1.2 copy.53
  220.4 2.0 copy.54
  222.5 10.5 %reshape.54 = bf16[16,32,2,32,32]{4,3,2,1,0:T(8,128)(2,1)} reshape(bf16[16,32,2048]{2,1,0:T(8,128)(2,1)} %param.7) | data formatting | bytes 4194304 | tf_op jit(solution)/shard_map/reshape | solution.py:91
  233.0 6.5 %slice_bitcast_fusion = (bf16[16,32,32,32]{3,2,1,0:T(8,128)(2,1)}, bf16[16,32,32,32]{3,2,1,0:T(8,128)(2,1)}) fusion(bf16[16,32,2,32,32]{4,3,2,1,0:T(8,128)(2,1)} %reshape.54), kind=kLoop, calls=%fused_computation.19 | loop fusion | bytes 4194304 | tf_op jit(solution)/shard_map/squeeze | solution.py:93
  239.5 53.6 %reduce-scatter.2.cloned.1.call-done = f32[32,16,128]{2,1,0:T(8,128)} async-done(((f32[256,16,128]{2,1,0:T(8,128)}), f32[32,16,128]{2,1,0:T(8,128)}) %reduce-scatter.2.cloned.1.call-update) | async-done | bytes 262160 | tf_op jit(solution)/shard_map/reduce_scatter | solution.py:82
  293.1 1.8 reshape.53
  294.9 8.9 %fusion.40 = f32[32,16,1,32]{3,2,1,0:T(1,128)S(1)} fusion(bf16[16,32,32,32]{3,2,1,0:T(8,128)(2,1)} %get-tuple-element.3, f32[32,16,2,2,32]{4,3,2,1,0:T(2,128)S(1)} %reshape.53), kind=kOutput, calls=%fused_computation.49 | convolution fusion | flops 6291456 | bytes 1376256 | tf_op jit(solution)/shard_map/mkio,kmo->kmi/dot_general | solution.py:94
  303.8 6.6 %fusion.38 = f32[32,16,1,32]{3,2,1,0:T(1,128)S(1)} fusion(bf16[16,32,32,32]{3,2,1,0:T(8,128)(2,1)S(1)} %copy-done.6, f32[32,16,2,2,32]{4,3,2,1,0:T(2,128)S(1)} %reshape.53), kind=kOutput, calls=%fused_computation.47 | convolution fusion | flops 6291456 | bytes 4521984 | tf_op jit(solution)/shard_map/mkio,kmo->kmi/dot_general | solution.py:97
  310.3 6.6 %fusion.36 = f32[32,16,1,32]{3,2,1,0:T(1,128)S(1)} fusion(bf16[16,32,32,32]{3,2,1,0:T(8,128)(2,1)S(1)} %copy-done.5, f32[32,16,2,2,32]{4,3,2,1,0:T(2,128)S(1)} %reshape.53), kind=kOutput, calls=%fused_computation.45 | convolution fusion | flops 6291456 | bytes 4521984 | tf_op jit(solution)/shard_map/mkio,kmo->kmi/dot_general | solution.py:94
  316.9 6.8 %fusion.34 = f32[32,16,1,32]{3,2,1,0:T(1,128)S(1)} fusion(bf16[16,32,32,32]{3,2,1,0:T(8,128)(2,1)S(1)} %copy-done.5, f32[32,16,2,2,32]{4,3,2,1,0:T(2,128)S(1)} %reshape.53), kind=kOutput, calls=%fused_computation.43 | convolution fusion | flops 6291456 | bytes 4521984 | tf_op jit(solution)/shard_map/mkio,kmo->kmi/dot_general | solution.py:97
  325.5 8.5 %all_to_all.15 = f32[32,16,1,128]{3,0,2,1:T(8,128)S(1)} all-to-all(f32[32,16,1,128]{3,0,2,1:T(8,128)S(1)} %copy.55), channel_id=1, replica_groups=mesh['dp'=4,'slab'=8] {'dp'}, dimensions={1} | all-to-all | bytes 524288 | tf_op jit(solution)/shard_map/all_to_all | solution.py:100
  336.0 3.5 fusion.69
  339.5 3.5 add_bitcast_fusion
  343.0 3.7 fusion.68
  346.6 3.5 subtract_bitcast_fusion
  350.8 2.7 copy.61
  353.5 4.4 reshape.52
  357.9 16.0 %all-gather.2.cloned.1.call-done = f32[256,16,64]{2,1,0:T(8,128)} async-done(((f32[32,16,64]{2,1,0:T(8,128)}), f32[256,16,64]{2,1,0:T(8,128)}) %all-gather.2.cloned.1.call-update) | async-done | bytes 1048592 | tf_op jit(solution)/shard_map/all_gather | solution.py:117
  373.9 2.9 copy.62
  377.5 1.5 fusion.66
  379.0 1.5 fusion.58
  380.5 2.4 copy.69
  383.0 3.4 copy.70
  386.4 7.4 %fusion.88 = f32[128,16,16,32]{0,1,3,2:T(8,128)} fusion(f32[16,16,16,32]{0,1,3,2:T(8,128)} %copy.70, s32[16]{0:T(128)S(1)} %compare_select_fusion), kind=kOutput, calls=%fused_computation.112 | convolution fusion | flops 201355264 | bytes 4718656 | tf_op jit(solution)/shard_map/mkxc,ym->xcyk/dot_general | solution.py:134
  393.8 5.2 fusion.94
  399.7 1.4 copy.65
  401.1 3.4 copy.66
  404.6 6.9 %fusion.96 = f32[128,16,16,32]{0,1,3,2:T(8,128)} fusion(f32[16,16,16,32]{0,1,3,2:T(8,128)} %copy.66, s32[16]{0:T(128)S(1)} %compare_select_fusion), kind=kOutput, calls=%fused_computation.120 | convolution fusion | flops 201355264 | bytes 4718656 | tf_op jit(solution)/shard_map/mkxc,ym->xcyk/dot_general | solution.py:134
  411.5 5.1 fusion.86
  416.6 54.8 %fusion.14 = f32[16,32,128,128]{3,2,1,0:T(8,128)S(1)} fusion(f32[128,16,16,32]{0,1,3,2:T(8,128)} %fusion.96, f32[128,16,16,32]{0,1,3,2:T(8,128)} %fusion.88), kind=kOutput, calls=%fused_computation.23 | convolution fusion | flops 1611689984 | bytes 41943040 | tf_op jit(solution)/shard_map/xcyk,zk->xcyz/dot_general | solution.py:140
  471.4 57.5 %fusion.8 = bf16[1,16,32,128,128]{4,3,2,1,0:T(8,128)(2,1)} fusion(f32[16,32,128,128]{3,2,1,0:T(8,128)S(1)} %fusion.14, f32[128,16,16,32]{0,1,3,2:T(8,128)} %fusion.94, f32[128,16,16,32]{0,1,3,2:T(8,128)} %fusion.86), kind=kOutput, calls=%fused_computation.13 | convolution fusion | flops 1628467200 | bytes 58720256 | tf_op jit(solution)/shard_map/xcyk,zk->xcyz/dot_general | solution.py:140
  (44 shorter events, 11.2 us)
Async XLA Ops:
  7.2 285.9 %reduce-scatter.2.cloned.1.call-start = ((), (), s32[]{:S(2)}) async-start(), calls=%async_computation.2 | async-start | bytes 2359296 | tf_op jit(solution)/shard_map/reduce_scatter | solution.py:82
  94.9 18.7 %copy-start.2 = (f32[16,32,128,16]{2,3,1,0:T(8,128)S(1)}, f32[16,32,128,16]{2,3,1,0:T(8,128)}, u32[]{:S(2)}) copy-start(f32[16,32,128,16]{2,3,1,0:T(8,128)} %fusion.45) | copy-start | bytes 12582916
  113.6 16.6 %copy-start = (f32[16,32,128,16]{2,3,1,0:T(8,128)S(1)}, f32[16,32,128,16]{2,3,1,0:T(8,128)}, u32[]{:S(2)}) copy-start(f32[16,32,128,16]{2,3,1,0:T(8,128)} %fusion.117) | copy-start | bytes 12582916
  113.6 16.6 %copy-start.7 = (f32[16,16,32,16]{2,0,3,1:T(8,128)S(1)}, f32[16,16,32,16]{2,0,3,1:T(8,128)}, u32[]{:S(2)}) copy-start(f32[16,16,32,16]{2,0,3,1:T(8,128)} %fusion.20) | copy-start | bytes 1572868
  146.8 16.6 %copy-start.1 = (f32[16,32,128,16]{2,3,1,0:T(8,128)S(1)}, f32[16,32,128,16]{2,3,1,0:T(8,128)}, u32[]{:S(2)}) copy-start(f32[16,32,128,16]{2,3,1,0:T(8,128)} %fusion.42) | copy-start | bytes 12582916
  222.4 151.5 %all-gather.2.cloned.1.call-start = ((), (), s32[]{:S(2)}) async-start(), calls=%async_computation.3 | async-start | bytes 2359296 | tf_op jit(solution)/shard_map/all_gather | solution.py:117
  294.9 8.9 %copy-start.6 = (bf16[16,32,32,32]{3,2,1,0:T(8,128)(2,1)S(1)}, bf16[16,32,32,32]{3,2,1,0:T(8,128)(2,1)}, u32[]{:S(2)}) copy-start(bf16[16,32,32,32]{3,2,1,0:T(8,128)(2,1)} %get-tuple-element.3) | copy-start | bytes 3145732
  294.9 15.5 %copy-start.5 = (bf16[16,32,32,32]{3,2,1,0:T(8,128)(2,1)S(1)}, bf16[16,32,32,32]{3,2,1,0:T(8,128)(2,1)}, u32[]{:S(2)}) copy-start(bf16[16,32,32,32]{3,2,1,0:T(8,128)(2,1)} %get-tuple-element.2) | copy-start | bytes 3145732
  316.9 8.5 %copy-start.9 = (f32[32,16,128]{2,1,0:T(8,128)S(1)}, f32[32,16,128]{2,1,0:T(8,128)}, u32[]{:S(2)}) copy-start(f32[32,16,128]{2,1,0:T(8,128)} %reduce-scatter.2.cloned.1.call-done) | copy-start | bytes 786436
  386.4 7.4 %copy-start.4 = (f32[16,16,16,32]{0,1,3,2:T(8,128)S(1)}, f32[16,16,16,32]{0,1,3,2:T(8,128)}, u32[]{:S(2)}) copy-start(f32[16,16,16,32]{0,1,3,2:T(8,128)} %copy.70) | copy-start | bytes 1572868
  393.8 5.2 copy-start.8
  404.6 6.9 %copy-start.3 = (f32[16,16,16,32]{0,1,3,2:T(8,128)S(1)}, f32[16,16,16,32]{0,1,3,2:T(8,128)}, u32[]{:S(2)}) copy-start(f32[16,16,16,32]{0,1,3,2:T(8,128)} %copy.66) | copy-start | bytes 1572868
Sparse Core Ops, SparseCore 0:
  222.5 70.4 reduce-scatter.1
  325.5 48.3 all-gather.1
where the time goes:
time: 540 us; the launch traced here: 536 us
  matrix products  359 us (66%)
  waiting for transfers between devices  69.6 us (13%)
  local copies, waits for them, and re-layouts  63.5 us (12%)
  other arithmetic  20.5 us (4%)
  between operations  14.6 us (3%)
  blocking collectives  8.48 us (2%)
    dot_general x1, matrix products, body(): jnp.einsum('xcyk,zk->xcyz', plane_imag, sin_z, precision=exact_mode)  57.5 us
    dot_general x1, matrix products, body(): jnp.einsum('xcyk,zk->xcyz', plane_real, cos_z, precision=exact_mode)  54.8 us
    reduce_scatter x1, waiting for transfers between devices, body(): lax.psum_scatter(jnp.stack([out_real, out_imag], axis=3).reshape(partial_...  53.6 us
    dot_general x2, matrix products, transform_planes(): jnp.einsum('xcyk,ym->mkxc', plane_imag, sin_y, precision=exact_mode)  36.5 us
    dot_general x2, matrix products, transform_planes(): jnp.einsum('xcyk,ym->mkxc', plane_real, sin_y, precision=exact_mode)  33.4 us
    dot_general x2, matrix products, transform_planes(): jnp.einsum('xcyk,ym->mkxc', plane_imag, cos_y, precision=exact_mode)  33 us
    dot_general x2, matrix products, transform_planes(): jnp.einsum('xcyk,ym->mkxc', plane_real, cos_y, precision=exact_mode)  32.9 us
    dot_general x2, matrix products, transform_planes(): jnp.einsum('xcyz,zk->xcyk', field, zcos_low, preferred_element_type=jnp.f...  18.4 us
  transfers between devices with their start and end apart: 2, of which 2 were waited for; matrix products, arithmetic and copies ran while one was open for 8% of the time, Pallas kernels for 0%

commit v1 on v0

v1 whole, which is shorter than its diff:
```python
import functools
import math

import jax
import jax.numpy as jnp
import numpy as np
import ml_dtypes
from jax import lax
from jax.experimental import pallas as pl
from jax.experimental.pallas import tpu as pltpu
from jax.sharding import PartitionSpec as P

C = 32
NX = 128
NY = 128
NZ = 128
MX = 16
MY = 16
MZ = 16
BF = ml_dtypes.bfloat16


def tables(length, freqs):
    product = np.arange(length)[:, None] * freqs[None, :] % length
    angle = product * (2.0 * math.pi / length)
    return np.cos(angle).astype(np.float32), np.sin(angle).astype(np.float32)


def signed(count):
    index = np.arange(count)
    return np.where(index < count // 2, index, index - count)


def halves(table):
    high = table.astype(BF)
    low = (table - high.astype(np.float32)).astype(BF)
    return high, low


COS_X, SIN_X = tables(NX, signed(MX))
COS_Y, SIN_Y = tables(NY, signed(MY))
COS_Z, SIN_Z = tables(NZ, np.arange(MZ))


def forward_tables():
    ty = np.concatenate([COS_Y.T, SIN_Y.T], 0)
    ty = np.concatenate(halves(ty), 0)
    zc = COS_Z.astype(BF).astype(np.float32).T
    zs = (-SIN_Z).astype(BF).astype(np.float32).T
    scale = (np.where(np.arange(MZ) == 0, 1.0, 2.0) / (NX * NY * NZ)).astype(np.float32)[:, None]
    zt = np.zeros((2, 2, MZ, 2, 2, NZ), np.float32)
    for field, factor in ((0, 1.0), (1, scale)):
        zt[field, 0, :, 0, field] = zc * factor
        zt[field, 0, :, 1, field] = zs * factor
        zt[field, 1, :, 0, field] = zs * factor
        zt[field, 1, :, 1, field] = -zc * factor
    return ty, zt.reshape(4 * MZ, 4 * NZ).astype(BF)


def inverse_tables():
    zi = np.zeros((2, MZ, 2, NZ), np.float32)
    zi[0, :, 0] = COS_Z.T
    zi[1, :, 0] = -SIN_Z.T
    zi[0, :, 1] = SIN_Z.T
    zi[1, :, 1] = COS_Z.T
    high, low = halves(zi.reshape(2 * MZ, 2 * NZ))
    zi = np.concatenate([high, high, low], 0)
    yl_high, yl_low = halves(np.concatenate([COS_Y, -SIN_Y], 1))
    yl = np.concatenate([yl_high, yl_high, yl_low], 1)
    return zi, yl


def split_f32(value):
    high = value.astype(jnp.bfloat16)
    low = (value - high.astype(jnp.float32)).astype(jnp.bfloat16)
    return high, low


def dot(a, b, dims=((1,), (0,))):
    return lax.dot_general(a, b, (dims, ((), ())), preferred_element_type=jnp.float32)


def gelu_slope(pre):
    return 0.5 * (1.0 + lax.erf(pre * (1.0 / math.sqrt(2.0)))) + pre * jnp.exp(-0.5 * pre * pre) * (
        1.0 / math.sqrt(2.0 * math.pi)
    )


def forward_kernel(planes, group, owned, cos_ref, sin_ref, ty_ref, zt_ref, u_ref, p_ref, g_ref, out_ref, rows, spec, acc):
    step = pl.program_id(0)

    @pl.when(step == 0)
    def _():
        acc[...] = jnp.zeros_like(acc)

    ty = ty_ref[...]
    for g in range(group):

        def channels(at, carry):
            for k in range(4):
                ch = at * 4 + k
                pre = p_ref[0, g, ch].astype(jnp.float32)
                gh = (g_ref[0, g, ch].astype(jnp.float32) * gelu_slope(pre)).astype(jnp.bfloat16)
                both = dot(ty, jnp.concatenate([u_ref[0, g, ch], gh], axis=1))
                both = both[: 2 * MY] + both[2 * MY :]
                for q in range(2):
                    for w in range(2):
                        rows[2 * q + w, pl.ds(ch, MY, stride=C), :] = both[
                            q * MY : (q + 1) * MY, w * NZ : (w + 1) * NZ
                        ]
            return carry

        lax.fori_loop(0, C // 4, channels, 0)
        high, low = split_f32(jnp.concatenate([rows[q] for q in range(4)], axis=1))
        nt = ((1,), (1,))
        spec[g] = dot(zt_ref[...], high, nt) + dot(zt_ref[...], low, nt)

    x0 = lax.axis_index("slab") * planes + step * group

    def modes(a, carry):
        for f in range(2):
            real = slice(f * 2 * MZ, f * 2 * MZ + MZ)
            imag = slice(f * 2 * MZ + MZ, f * 2 * MZ + 2 * MZ)
            sum_r, sum_i = acc[a, real], acc[a, imag]
            for g in range(group):
                c = cos_ref[(x0 + g) * MX + a]
                s = sin_ref[(x0 + g) * MX + a]
                br, bi = spec[g, real], spec[g, imag]
                sum_r = sum_r + (br * c + bi * s)
                sum_i = sum_i + (bi * c - br * s)
            acc[a, real] = sum_r
            acc[a, imag] = sum_i
        return carry

    lax.fori_loop(0, MX, modes, 0)

    @pl.when(step == pl.num_programs(0) - 1)
    def _():
        size = min(MZ, owned)

        def shuffle(a, carry):
            for b in range(MY):
                part = jnp.concatenate(
                    [acc[a, q * MZ : (q + 1) * MZ, b * C : (b + 1) * C] for q in range(4)], axis=1
                )
                for j in range(0, MZ, size):
                    row = b * MZ + j
                    out_ref[row // owned, a, row % owned : row % owned + size] = part[j : j + size]
            return carry

        lax.fori_loop(0, MX, shuffle, 0)


def mode_kernel(owned, x_ref, w_ref, e_ref, out_ref):
    half = owned // 2
    gr = x_ref[:, 2 * C : 3 * C]
    gi = x_ref[:, 3 * C : 4 * C]
    gr = jnp.concatenate([gr] * 4, axis=1)
    gi = jnp.concatenate([gi] * 4, axis=1)
    total = None
    width = C * C
    for k in range(width // 128):
        wr = w_ref[:, k * 128 : (k + 1) * 128].astype(jnp.float32)
        wi = w_ref[:, width + k * 128 : width + (k + 1) * 128].astype(jnp.float32)
        both = jnp.concatenate([wr * gr + wi * gi, wr * gi - wi * gr], axis=1)
        high, low = split_f32(both)
        part = dot(high, e_ref[k]) + dot(low, e_ref[k])
        total = part if total is None else total + part
    for a in range(out_ref.shape[0]):
        mine = total[a * owned : (a + 1) * owned]
        out_ref[a] = jnp.concatenate([mine[:half], mine[half:]], axis=1)


def gradient_kernel(x_ref, e_ref, out_ref):
    samples = x_ref.shape[0]
    width = C * C
    tiled = []
    for s in range(samples):
        high, low = split_f32(x_ref[s, :, : 2 * C])
        gr = jnp.concatenate([x_ref[s, :, 2 * C : 3 * C]] * 4, axis=1)
        gi = jnp.concatenate([x_ref[s, :, 3 * C : 4 * C]] * 4, axis=1)
        tiled.append((high, low, gr, gi))
    for k in range(width // 128):
        real = imag = None
        for high, low, gr, gi in tiled:
            wide = dot(high, e_ref[k]) + dot(low, e_ref[k])
            ur, ui = wide[:, :128], wide[:, 128:]
            r, i = ur * gr + ui * gi, ur * gi - ui * gr
            real = r if real is None else real + r
            imag = i if imag is None else imag + i
        out_ref[:, k * 128 : (k + 1) * 128] = real
        out_ref[:, width + k * 128 : width + (k + 1) * 128] = imag


def inverse_kernel(planes, group, owned, cos_ref, sin_ref, zi_ref, yl_ref, d_ref, out_ref, modes, mid):
    step = pl.program_id(0)
    half = owned // 2

    @pl.when(step == 0)
    def _():
        def unpack(a, carry):
            for s in range(d_ref.shape[0]):
                for h in range(2):
                    row = s * owned + h * half
                    for j in range(0, half, min(half, MZ)):
                        b, c = (row + j) // MZ, (row + j) % MZ
                        size = min(half, MZ)
                        for q in range(2):
                            modes[a, q * MZ + c : q * MZ + c + size, b * C : (b + 1) * C] = d_ref[
                                s, a, j : j + size, h * 2 * C + q * C : h * 2 * C + (q + 1) * C
                            ]
            return carry

        lax.fori_loop(0, MX, unpack, 0)

    x0 = lax.axis_index("slab") * planes + step * group
    yl = yl_ref[...]
    for g in range(group):

        def add(a, carry):
            real, imag = carry
            c = cos_ref[(x0 + g) * MX + a]
            s = sin_ref[(x0 + g) * MX + a]
            ur, ui = modes[a, :MZ], modes[a, MZ:]
            return real + (ur * c - ui * s), imag + (ui * c + ur * s)

        zero = jnp.zeros((MZ, MY * C), jnp.float32)
        real, imag = lax.fori_loop(0, MX, add, (zero, zero))
        high, low = split_f32(jnp.concatenate([real, imag], axis=0))
        both = dot(jnp.concatenate([high, low, high], axis=0), zi_ref[...], ((0,), (0,)))
        mid[0] = both[:, :NZ]
        mid[1] = both[:, NZ:]

        def channels(at, carry):
            for k in range(4):
                ch = at * 8 + 2 * k
                parts = [
                    [
                        mid[q, pl.ds(ch + n, MY, stride=C), :]
                        for n in range(2)
                    ]
                    for q in range(2)
                ]
                wide = jnp.concatenate([jnp.concatenate(p, axis=1) for p in parts], axis=0)
                high, low = split_f32(wide)
                result = dot(yl, jnp.concatenate([high, low, high], axis=0)).astype(jnp.bfloat16)
                out_ref[0, g, ch] = result[:, :NZ]
                out_ref[0, g, ch + 1] = result[:, NZ:]
            return carry

        lax.fori_loop(0, C // 8, channels, 0)


def sum_table():
    e = np.zeros((8, 2, 4, C, 2, C), np.float32)
    for k in range(8):
        for q in range(2):
            for j in range(4):
                e[k, q, j, :, q, 4 * k + j] = 1.0
    return e.reshape(8, 256, 2 * C).astype(BF)


VMEM = pl.BlockSpec(memory_space=pltpu.VMEM)
SMEM = pl.BlockSpec(memory_space=pltpu.SMEM)


def whole(array):
    rank = len(array.shape)
    return pl.BlockSpec(array.shape, lambda i: (0,) * rank)


def body(u_field, preact, cotangent, weights):
    planes = u_field.shape[1]
    slabs = lax.axis_size("slab")
    dps = lax.axis_size("dp")
    owned = MY * MZ // slabs
    group = min(2, planes)
    cos_x, sin_x = jnp.asarray(COS_X.reshape(-1)), jnp.asarray(SIN_X.reshape(-1))
    ty, zt = (jnp.asarray(t) for t in forward_tables())
    zi, yl = (jnp.asarray(t) for t in inverse_tables())
    table = sum_table()
    e_sum = jnp.asarray(table)
    e_wide = jnp.asarray(np.ascontiguousarray(table.transpose(0, 2, 1)))
    field_spec = pl.BlockSpec((1, group, C, NY, NZ), lambda i: (0, i, 0, 0, 0))
    params = pltpu.CompilerParams(vmem_limit_bytes=50 * 2**20)

    partial = pl.pallas_call(
        functools.partial(forward_kernel, planes, group, owned),
        grid=(planes // group,),
        in_specs=[SMEM, SMEM, whole(ty), whole(zt), field_spec, field_spec, field_spec],
        out_specs=pl.BlockSpec((slabs, MX, owned, 4 * C), lambda i: (0, 0, 0, 0)),
        out_shape=jax.ShapeDtypeStruct((slabs, MX, owned, 4 * C), jnp.float32),
        scratch_shapes=[
            pltpu.VMEM((4, MY * C, NZ), jnp.float32),
            pltpu.VMEM((group, 4 * MZ, MY * C), jnp.float32),
            pltpu.VMEM((MX, 4 * MZ, MY * C), jnp.float32),
        ],
        compiler_params=params,
    )(cos_x, sin_x, ty, zt, u_field, preact, cotangent)

    own = lax.psum_scatter(partial, "slab", scatter_dimension=0, tiled=True)[0]
    rows = MX * owned
    cut = 4
    back = pl.pallas_call(
        functools.partial(mode_kernel, owned),
        grid=(cut,),
        in_specs=[
            pl.BlockSpec((rows // cut, 4 * C), lambda i: (i, 0)),
            pl.BlockSpec((rows // cut, 2 * C * C), lambda i: (i, 0)),
            whole(e_sum),
        ],
        out_specs=pl.BlockSpec((MX // cut, owned // 2, 4 * C), lambda i: (i, 0, 0)),
        out_shape=jax.ShapeDtypeStruct((MX, owned // 2, 4 * C), jnp.float32),
        compiler_params=params,
    )(own.reshape(rows, 4 * C), weights.reshape(rows, 2 * C * C), e_sum)
    spread = lax.all_gather(back, "slab", axis=0, tiled=False)

    share = MX // dps
    swapped = lax.all_to_all(
        own.reshape(dps, share, owned, 4 * C), "dp", split_axis=0, concat_axis=0, tiled=True
    ).reshape(dps, share * owned, 4 * C)
    grad_weights = pl.pallas_call(
        gradient_kernel,
        in_specs=[VMEM, VMEM],
        out_specs=VMEM,
        out_shape=jax.ShapeDtypeStruct((share * owned, 2 * C * C), jnp.float32),
        compiler_params=params,
    )(swapped, e_wide).reshape(share, owned, 2 * C * C)

    grad_field = pl.pallas_call(
        functools.partial(inverse_kernel, planes, group, owned),
        grid=(planes // group,),
        in_specs=[SMEM, SMEM, whole(zi), whole(yl), whole(spread)],
        out_specs=field_spec,
        out_shape=jax.ShapeDtypeStruct((1, planes, C, NY, NZ), jnp.bfloat16),
        scratch_shapes=[
            pltpu.VMEM((MX, 2 * MZ, MY * C), jnp.float32),
            pltpu.VMEM((2, MY * C, NZ), jnp.float32),
        ],
        compiler_params=params,
    )(cos_x, sin_x, zi, yl, spread)
    return grad_weights, grad_field


def solution(mesh):
    placed = (
        P("dp", "slab", None, None, None),
        P("dp", "slab", None, None, None),
        P("dp", "slab", None, None, None),
        P(None, "slab", None),
    )
    return jax.shard_map(
        body,
        mesh=mesh,
        in_specs=placed,
        out_specs=(P("dp", "slab", None), P("dp", "slab", None, None, None)),
        check_vma=False,
    )
```

time: 540 us -> 222 us (0.41)
  matrix products: 359 us -> 0 us
  Pallas kernels: 0 us -> 94.6 us
  local copies, waits for them, and re-layouts: 63.5 us -> 5.3 us
  waiting for transfers between devices: 69.6 us -> 98.2 us
  other arithmetic: 20.5 us -> 0 us
    dot_general x34 -> x0, matrix products: 359 us -> none  [the longest x1 57.5 us: body(): jnp.einsum('xcyk,zk->xcyz', plane_imag, sin_z, precision=exact_mode)]
    pallas_call x0 -> x4, Pallas kernels: none -> 94.6 us  [the longest x1 60.4 us: body(): pl.pallas_call(functools.partial(forward_kernel, planes, group, owned), g...]
    reshape x6 -> x0, local copies, waits for them, and re-layouts: 20.6 us -> none  [the longest x1 10.5 us: body(): split_weights = weights.astype(jnp.float32).reshape(MX, owned_rows, 2, C, C)]
    convert_element_type x1 -> x0, other arithmetic: 18.2 us -> none  [body(): grad_out = (cotangent[0].astype(jnp.float32) * slope).astype(jnp.bfloat16)]
    reduce_scatter x1, waiting for transfers between devices: 53.6 us -> 70.5 us  [body(): own = lax.psum_scatter(partial, 'slab', scatter_dimension=0, tiled=True)[0]]
    squeeze x3 -> x0, local copies, waits for them, and re-layouts: 13.4 us -> none  [the longest x1 6.5 us: body(): weight_imag = split_weights[:, :, 1]]
    all_gather x1, waiting for transfers between devices: 16 us -> 27.6 us  [body(): spread = lax.all_gather(back, 'slab', axis=0, tiled=False)]
    another operation x3 -> x0, local copies, waits for them, and re-layouts: 8.73 us -> none  [the longest x1 4.86 us: body(): jnp.stack([ub_real, ub_imag, gb_real, gb_imag], axis=3)]
  transfers between devices with their start and end apart: 2 -> 2, of which waited for: 2 -> 2; matrix products, arithmetic and copies ran while one was open for 8% -> 0% of each run, Pallas kernels for 0% -> 1%
where the time goes in v1:
time: 222 us
  waiting for transfers between devices  98.2 us (44%)
  Pallas kernels  94.6 us (43%)
  between operations  14.1 us (6%)
  blocking collectives  9.42 us (4%)
  local copies, waits for them, and re-layouts  5.3 us (2%)
    reduce_scatter x1, waiting for transfers between devices, body(): own = lax.psum_scatter(partial, 'slab', scatter_dimension=0, tiled=True)[0]  70.5 us
    pallas_call x1, Pallas kernels, body(): pl.pallas_call(functools.partial(forward_kernel, planes, group, owned), g...  60.4 us
    pallas_call x1, Pallas kernels, body(): pl.pallas_call(functools.partial(inverse_kernel, planes, group, owned), g...  29 us
    all_gather x1, waiting for transfers between devices, body(): spread = lax.all_gather(back, 'slab', axis=0, tiled=False)  27.6 us
    all_to_all x1, blocking collectives, body(): lax.all_to_all(own.reshape(dps, share, owned, 4 * C), 'dp', split_axis=0,...  9.42 us
    unnamed x26, local copies, waits for them, and re-layouts  5.3 us
  transfers between devices with their start and end apart: 2, of which 2 were waited for; matrix products, arithmetic and copies ran while one was open for 0% of the time, Pallas kernels for 1%

profile of v1, /device:TPU:0, one launch (start us, length us, event | category | flops | bytes accessed | tf_op | source)
XLA Modules:
  0.0 221.6 jit_solution(12546103384225387081)
XLA Ops:
  7.2 0.0 copy-start.3
  7.2 0.0 copy-start.4
  7.2 0.0 copy-start
  7.2 0.0 reduce-scatter.2.cloned.1.call-start
  7.2 0.0 copy-start.5
  7.3 1.0 copy-done.5
  8.2 0.0 copy-start.8
  8.2 0.7 copy-done.8
  8.9 0.0 copy-start.10
  8.9 0.7 copy-done.10
  9.6 0.0 copy-start.12
  9.6 0.7 copy-done.12
  10.4 0.0 copy-start.6
  10.4 0.0 copy-start.7
  10.4 0.0 copy-start.9
  10.4 0.0 copy-start.11
  10.4 60.4 %shard_map.131 = f32[8,16,32,128]{3,2,1,0:T(8,128)} custom-call(f32[2048]{0:T(1024)S(1)} %copy-done.8, f32[2048]{0:T(1024)S(1)} %copy-done.10, bf16[64,128]{1,0:T(8,128)(2,1)S(1)} %copy-done.12, bf16[64,512]{1,0:T(8,128)(2,1)S(1)} %copy-done.5, bf16[1,16,32,128,128]{4,3,2,1,0:T(8,128)(2,1)} %u_ref.1, bf16[1,16,32,128,128]{4,3,2,1,0:T(8,128)(2,1)} %p_ref.1, ...), custom_call_target="tpu_custom_call" | custom-call | tf_op jit(solution)/shard_map/pallas_call | solution.py:287
  70.7 0.0 reduce-scatter.2.cloned.1.call-update
  70.8 0.0 all-gather.3.cloned.1.call-start
  70.8 70.5 %reduce-scatter.2.cloned.1.call-done = f32[1,16,32,128]{3,2,1,0:T(8,128)} async-done(((f32[8,16,32,128]{3,2,1,0:T(8,128)}), f32[1,16,32,128]{3,2,1,0:T(8,128)}) %reduce-scatter.2.cloned.1.call-update) | async-done | bytes 262160 | tf_op jit(solution)/shard_map/reduce_scatter | solution.py:301
  141.4 0.0 copy-done.3
  141.4 0.0 copy-done
  141.4 0.0 copy-start.2
  141.4 0.9 copy-done.2
  142.3 3.0 %shard_map.133 = f32[16,16,128]{2,1,0:T(8,128)} custom-call(f32[512,128]{1,0:T(8,128)S(1)} %bitcast.9, bf16[512,2048]{1,0:T(8,128)(2,1)S(1)} %bitcast.6, bf16[8,256,64]{2,1,0:T(8,128)(2,1)S(1)} %copy-done.3), custom_call_target="tpu_custom_call" | custom-call | tf_op jit(solution)/shard_map/pallas_call | solution.py:304
  145.3 0.0 all-gather.3.cloned.1.call-update
  145.3 9.4 %all_to_all.5 = f32[4,4,32,128]{3,2,1,0:T(8,128)S(1)} all-to-all(f32[4,4,32,128]{3,2,1,0:T(8,128)} %bitcast.8), channel_id=1, replica_groups=mesh['dp'=4,'slab'=8] {'dp'}, dimensions={0} | all-to-all | bytes 524288 | tf_op jit(solution)/shard_map/all_to_all | solution.py:319
  154.7 0.0 copy-done.4
  154.7 2.2 %shard_map.132 = f32[128,2048]{1,0:T(8,128)} custom-call(f32[4,128,128]{2,1,0:T(8,128)S(1)} %bitcast.10, bf16[8,64,256]{2,1,0:T(8,128)(2,1)S(1)} %copy-done.4), custom_call_target="tpu_custom_call" | custom-call | tf_op jit(solution)/shard_map/pallas_call | solution.py:322
  157.0 27.6 %all-gather.3.cloned.1.call-done = f32[128,16,128]{2,1,0:T(8,128)} async-done(((f32[16,16,128]{2,1,0:T(8,128)}), f32[128,16,128]{2,1,0:T(8,128)}) %all-gather.3.cloned.1.call-update) | async-done | bytes 1048592 | tf_op jit(solution)/shard_map/all_gather | solution.py:316
  184.6 0.0 copy-done.6
  184.6 0.0 copy-done.7
  184.6 0.0 copy-done.9
  184.6 0.0 copy-done.11
  184.6 0.0 copy-start.1
  184.6 1.2 copy-done.1
  185.8 29.0 %shard_map.134 = bf16[1,16,32,128,128]{4,3,2,1,0:T(8,128)(2,1)} custom-call(f32[2048]{0:T(1024)S(1)} %copy-done.9, f32[2048]{0:T(1024)S(1)} %copy-done.11, bf16[96,256]{1,0:T(8,128)(2,1)S(1)} %copy-done.6, bf16[128,96]{1,0:T(8,128)(2,1)S(1)} %copy-done.7, f32[8,16,16,128]{3,2,1,0:T(8,128)S(1)} %bitcast.7), custom_call_target="tpu_custom_call" | custom-call | tf_op jit(solution)/shard_map/pallas_call | solution.py:330
Async XLA Ops:
  7.2 134.2 %copy-start.3 = (bf16[8,256,64]{2,1,0:T(8,128)(2,1)S(1)}, bf16[8,256,64]{2,1,0:T(8,128)(2,1)}, u32[]{:S(2)}) copy-start(bf16[8,256,64]{2,1,0:T(8,128)(2,1)} %constant.22.clone.e_ref) | copy-start | bytes 786436
  7.2 147.6 %copy-start.4 = (bf16[8,64,256]{2,1,0:T(8,128)(2,1)S(1)}, bf16[8,64,256]{2,1,0:T(8,128)(2,1)}, u32[]{:S(2)}) copy-start(bf16[8,64,256]{2,1,0:T(8,128)(2,1)} %constant.23.clone.e_ref) | copy-start | bytes 786436
  7.2 134.2 %copy-start = (bf16[16,32,2048]{2,1,0:T(8,128)(2,1)S(1)}, bf16[16,32,2048]{2,1,0:T(8,128)(2,1)}, u32[]{:S(2)}) copy-start(bf16[16,32,2048]{2,1,0:T(8,128)(2,1)} %param.15) | copy-start | bytes 6291460
  7.2 134.2 %reduce-scatter.2.cloned.1.call-start = ((), (), s32[]{:S(2)}) async-start(), calls=%async_computation.2 | async-start | bytes 2359296 | tf_op jit(solution)/shard_map/reduce_scatter | solution.py:301
  7.2 1.0 copy-start.5
  8.2 0.7 copy-start.8
  8.9 0.7 copy-start.10
  9.6 0.7 copy-start.12
  10.4 174.2 %copy-start.6 = (bf16[96,256]{1,0:T(8,128)(2,1)S(1)}, bf16[96,256]{1,0:T(8,128)(2,1)}, u32[]{:S(2)}) copy-start(bf16[96,256]{1,0:T(8,128)(2,1)} %constant.20.clone.zi_ref) | copy-start | bytes 147460
  10.4 174.2 %copy-start.7 = (bf16[128,96]{1,0:T(8,128)(2,1)S(1)}, bf16[128,96]{1,0:T(8,128)(2,1)}, u32[]{:S(2)}) copy-start(bf16[128,96]{1,0:T(8,128)(2,1)} %constant.21.clone.yl_ref) | copy-start | bytes 73732
  10.4 174.2 %copy-start.9 = (f32[2048]{0:T(1024)S(1)}, f32[2048]{0:T(1024)}, u32[]{:S(2)}) copy-start(f32[2048]{0:T(1024)} %constant.16.clone.cos_ref) | copy-start | bytes 24580
  10.4 174.2 %copy-start.11 = (f32[2048]{0:T(1024)S(1)}, f32[2048]{0:T(1024)}, u32[]{:S(2)}) copy-start(f32[2048]{0:T(1024)} %constant.17.clone.sin_ref) | copy-start | bytes 24580
  70.8 113.8 %all-gather.3.cloned.1.call-start = ((), (), s32[]{:S(2)}) async-start(), calls=%async_computation.3 | async-start | bytes 1179648 | tf_op jit(solution)/shard_map/all_gather | solution.py:316
  141.4 1.0 copy-start.2
  184.6 1.2 copy-start.1
Sparse Core Ops, SparseCore 0:
  70.9 70.4 reduce-scatter.1
  145.4 39.1 all-gather.2

commit v2 on v1

--- a/solution.py
+++ b/solution.py
@@ -86,19 +86,49 @@
     )
 
 
-def forward_kernel(planes, group, owned, cos_ref, sin_ref, ty_ref, zt_ref, u_ref, p_ref, g_ref, out_ref, rows, spec, acc):
+def quarter_turn(value):
+    q = [value[..., k * C : (k + 1) * C] for k in range(4)]
+    return jnp.concatenate([q[1], -q[0], q[3], -q[2]], axis=-1)
+
+
+def forward_kernel(planes, group, owned, slabs, cos_ref, sin_ref, ty_ref, zt_ref, u_ref, p_ref, g_ref, out_ref, rows, send, held, send_sem, recv_sem):
     step = pl.program_id(0)
+    steps = planes // group
+    me = lax.axis_index("slab")
+
+    def peer(k):
+        return lax.rem(me + k, slabs)
+
+    def copy(at, k_to, k_from):
+        return pltpu.make_async_remote_copy(
+            src_ref=send.at[at, k_to],
+            dst_ref=held.at[at, k_from],
+            send_sem=send_sem.at[at, k_to],
+            recv_sem=recv_sem.at[at, k_from],
+            device_id=(lax.axis_index("dp"), k_to),
+            device_id_type=pl.DeviceIdType.MESH,
+        )
+
+    barrier = pltpu.get_barrier_semaphore()
 
     @pl.when(step == 0)
     def _():
-        acc[...] = jnp.zeros_like(acc)
+        def greet(k, carry):
+            pl.semaphore_signal(
+                barrier, inc=1, device_id=(lax.axis_index("dp"), peer(k)), device_id_type=pl.DeviceIdType.MESH
+            )
+            return carry
+
+        lax.fori_loop(1, slabs, greet, 0)
 
     ty = ty_ref[...]
+    size = min(MZ, owned)
+    unroll = 16
     for g in range(group):
 
         def channels(at, carry):
-            for k in range(4):
-                ch = at * 4 + k
+            for k in range(unroll):
+                ch = at * unroll + k
                 pre = p_ref[0, g, ch].astype(jnp.float32)
                 gh = (g_ref[0, g, ch].astype(jnp.float32) * gelu_slope(pre)).astype(jnp.bfloat16)
                 both = dot(ty, jnp.concatenate([u_ref[0, g, ch], gh], axis=1))
@@ -110,45 +140,68 @@
                         ]
             return carry
 
-        lax.fori_loop(0, C // 4, channels, 0)
+        lax.fori_loop(0, C // unroll, channels, 0)
         high, low = split_f32(jnp.concatenate([rows[q] for q in range(4)], axis=1))
         nt = ((1,), (1,))
-        spec[g] = dot(zt_ref[...], high, nt) + dot(zt_ref[...], low, nt)
-
-    x0 = lax.axis_index("slab") * planes + step * group
-
-    def modes(a, carry):
-        for f in range(2):
-            real = slice(f * 2 * MZ, f * 2 * MZ + MZ)
-            imag = slice(f * 2 * MZ + MZ, f * 2 * MZ + 2 * MZ)
-            sum_r, sum_i = acc[a, real], acc[a, imag]
-            for g in range(group):
-                c = cos_ref[(x0 + g) * MX + a]
-                s = sin_ref[(x0 + g) * MX + a]
-                br, bi = spec[g, real], spec[g, imag]
-                sum_r = sum_r + (br * c + bi * s)
-                sum_i = sum_i + (bi * c - br * s)
-            acc[a, real] = sum_r
-            acc[a, imag] = sum_i
+        spec = dot(zt_ref[...], high, nt) + dot(zt_ref[...], low, nt)
+        for b in range(MY):
+            part = jnp.concatenate(
+                [spec[q * MZ : (q + 1) * MZ, b * C : (b + 1) * C] for q in range(4)], axis=1
+            )
+            for j in range(0, MZ, size):
+                row = b * MZ + j
+                send[step, row // owned, g, row % owned : row % owned + size] = part[j : j + size]
+
+    @pl.when(step == 0)
+    def _():
+        pl.semaphore_wait(barrier, slabs - 1)
+
+    def push(k, carry):
+        copy(step, peer(k), me).start()
         return carry
 
-    lax.fori_loop(0, MX, modes, 0)
-
-    @pl.when(step == pl.num_programs(0) - 1)
+    lax.fori_loop(1, slabs, push, 0)
+    held[step, me] = send[step, me]
+
+    @pl.when(step == steps - 1)
     def _():
-        size = min(MZ, owned)
-
-        def shuffle(a, carry):
-            for b in range(MY):
-                part = jnp.concatenate(
-                    [acc[a, q * MZ : (q + 1) * MZ, b * C : (b + 1) * C] for q in range(4)], axis=1
-                )
-                for j in range(0, MZ, size):
-                    row = b * MZ + j
-                    out_ref[row // owned, a, row % owned : row % owned + size] = part[j : j + size]
-            return carry
-
-        lax.fori_loop(0, MX, shuffle, 0)
+        for at in range(steps):
+
+            def arrive(k, carry):
+                copy(at, peer(k), peer(k)).wait_recv()
+                return carry
+
+            lax.fori_loop(1, slabs, arrive, 0)
+
+        for low, high in ((0, 5), (5, MX // 2 + 1)):
+
+            def planes_of(src, totals):
+                totals = list(totals)
+                for at in range(steps):
+                    for g in range(group):
+                        value = held[at, src, g]
+                        x = (src * planes + at * group + g) * MX
+                        for n, f in enumerate(range(low, high)):
+                            totals[2 * n] = totals[2 * n] + value * cos_ref[x + f]
+                            if f:
+                                totals[2 * n + 1] = totals[2 * n + 1] + value * sin_ref[x + f]
+                return tuple(totals)
+
+            zero = jnp.zeros((owned, 4 * C), jnp.float32)
+            totals = lax.fori_loop(0, slabs, planes_of, (zero,) * (2 * (high - low)))
+            for n, f in enumerate(range(low, high)):
+                turned = quarter_turn(totals[2 * n + 1])
+                out_ref[f] = totals[2 * n] + turned
+                if 0 < f < MX // 2:
+                    out_ref[MX - f] = totals[2 * n] - turned
+
+        for at in range(steps):
+
+            def sent(k, carry):
+                copy(at, peer(k), me).wait_send()
+                return carry
+
+            lax.fori_loop(1, slabs, sent, 0)
 
 
 def mode_kernel(owned, x_ref, w_ref, e_ref, out_ref):
@@ -232,8 +285,8 @@
         mid[1] = both[:, NZ:]
 
         def channels(at, carry):
-            for k in range(4):
-                ch = at * 8 + 2 * k
+            for k in range(8):
+                ch = at * 16 + 2 * k
                 parts = [
                     [
                         mid[q, pl.ds(ch + n, MY, stride=C), :]
@@ -248,7 +301,7 @@
                 out_ref[0, g, ch + 1] = result[:, NZ:]
             return carry
 
-        lax.fori_loop(0, C // 8, channels, 0)
+        lax.fori_loop(0, C // 16, channels, 0)
 
 
 def sum_table():
@@ -284,21 +337,25 @@
     field_spec = pl.BlockSpec((1, group, C, NY, NZ), lambda i: (0, i, 0, 0, 0))
     params = pltpu.CompilerParams(vmem_limit_bytes=50 * 2**20)
 
-    partial = pl.pallas_call(
-        functools.partial(forward_kernel, planes, group, owned),
-        grid=(planes // group,),
+    steps = planes // group
+    own = pl.pallas_call(
+        functools.partial(forward_kernel, planes, group, owned, slabs),
+        grid=(steps,),
         in_specs=[SMEM, SMEM, whole(ty), whole(zt), field_spec, field_spec, field_spec],
-        out_specs=pl.BlockSpec((slabs, MX, owned, 4 * C), lambda i: (0, 0, 0, 0)),
-        out_shape=jax.ShapeDtypeStruct((slabs, MX, owned, 4 * C), jnp.float32),
+        out_specs=pl.BlockSpec((MX, owned, 4 * C), lambda i: (0, 0, 0)),
+        out_shape=jax.ShapeDtypeStruct((MX, owned, 4 * C), jnp.float32),
         scratch_shapes=[
             pltpu.VMEM((4, MY * C, NZ), jnp.float32),
-            pltpu.VMEM((group, 4 * MZ, MY * C), jnp.float32),
-            pltpu.VMEM((MX, 4 * MZ, MY * C), jnp.float32),
+            pltpu.VMEM((steps, slabs, group, owned, 4 * C), jnp.float32),
+            pltpu.VMEM((steps, slabs, group, owned, 4 * C), jnp.float32),
+            pltpu.SemaphoreType.DMA((steps, slabs)),
+            pltpu.SemaphoreType.DMA((steps, slabs)),
         ],
-        compiler_params=params,
+        compiler_params=pltpu.CompilerParams(
+            vmem_limit_bytes=50 * 2**20, collective_id=0, has_side_effects=True
+        ),
     )(cos_x, sin_x, ty, zt, u_field, preact, cotangent)
 
-    own = lax.psum_scatter(partial, "slab", scatter_dimension=0, tiled=True)[0]
     rows = MX * owned
     cut = 4
     back = pl.pallas_call(

time: 222 us -> 147 us (0.66)
  waiting for transfers between devices: 98.2 us -> 29.1 us
  Pallas kernels: 94.6 us -> 90.4 us
    reduce_scatter x1 -> x0, waiting for transfers between devices: 70.5 us -> none  [body(): own = lax.psum_scatter(partial, 'slab', scatter_dimension=0, tiled=True)[0]]
    pallas_call x1, Pallas kernels: 29 us -> 23.4 us  [body(): pl.pallas_call(functools.partial(inverse_kernel, planes, group, owned), g...]
    unnamed x26 -> x24, local copies, waits for them, and re-layouts: 5.3 us -> 4.35 us
  transfers between devices with their start and end apart: 2 -> 1, of which waited for: 2 -> 1; matrix products, arithmetic and copies ran while one was open for 0% -> 0% of each run, Pallas kernels for 1% -> 2%
where the time goes in v2:
time: 147 us
  Pallas kernels  90.4 us (61%)
  waiting for transfers between devices  29.1 us (20%)
  between operations  14.1 us (10%)
  blocking collectives  8.63 us (6%)
  local copies, waits for them, and re-layouts  4.35 us (3%)
    pallas_call x1, Pallas kernels, body(): pl.pallas_call(functools.partial(forward_kernel, planes, group, owned, sl...  61.8 us
    all_gather x1, waiting for transfers between devices, body(): spread = lax.all_gather(back, 'slab', axis=0, tiled=False)  29.1 us
    pallas_call x1, Pallas kernels, body(): pl.pallas_call(functools.partial(inverse_kernel, planes, group, owned), g...  23.4 us
    all_to_all x1, blocking collectives, body(): lax.all_to_all(own.reshape(dps, share, owned, 4 * C), 'dp', split_axis=0,...  8.63 us
    unnamed x24, local copies, waits for them, and re-layouts  4.35 us
    pallas_call x1, Pallas kernels, body(): pl.pallas_call(functools.partial(mode_kernel, owned), grid=(cut,), in_spe...  3 us
  transfers between devices with their start and end apart: 1, of which 1 were waited for; matrix products, arithmetic and copies ran while one was open for 0% of the time, Pallas kernels for 2%

profile of v2, /device:TPU:0, one launch (start us, length us, event | category | flops | bytes accessed | tf_op | source)
XLA Modules:
  0.0 146.6 jit_solution(2274857029905817218)
XLA Ops:
  7.2 0.0 copy-start.2
  7.2 0.0 copy-start.3
  7.2 0.0 copy-start
  7.2 0.0 all-gather.3.cloned.1.call-start
  7.2 0.0 copy-start.4
  7.3 1.0 copy-done.4
  8.2 0.0 copy-start.7
  8.2 0.7 copy-done.7
  8.9 0.0 copy-start.9
  8.9 0.7 copy-done.9
  9.6 0.0 copy-start.11
  9.6 0.7 copy-done.11
  10.4 0.0 copy-start.5
  10.4 0.0 copy-start.6
  10.4 0.0 copy-start.8
  10.4 0.0 copy-start.10
  10.4 61.8 %shard_map.131 = f32[16,32,128]{2,1,0:T(8,128)S(1)} custom-call(f32[2048]{0:T(1024)S(1)} %copy-done.7, f32[2048]{0:T(1024)S(1)} %copy-done.9, bf16[64,128]{1,0:T(8,128)(2,1)S(1)} %copy-done.11, bf16[64,512]{1,0:T(8,128)(2,1)S(1)} %copy-done.4, bf16[1,16,32,128,128]{4,3,2,1,0:T(8,128)(2,1)} %u_ref.1, bf16[1,16,32,128,128]{4,3,2,1,0:T(8,128)(2,1)} %p_ref.1, ...), custom_call_target="tpu_custom_call" | custom-call | tf_op jit(solution)/shard_map/pallas_call | solution.py:341
  72.1 0.0 copy-done.2
  72.1 0.0 copy-done
  72.1 3.0 %shard_map.133 = f32[16,16,128]{2,1,0:T(8,128)} custom-call(f32[512,128]{1,0:T(8,128)S(1)} %bitcast.6, bf16[512,2048]{1,0:T(8,128)(2,1)S(1)} %bitcast.8, bf16[8,256,64]{2,1,0:T(8,128)(2,1)S(1)} %copy-done.2), custom_call_target="tpu_custom_call" | custom-call | tf_op jit(solution)/shard_map/pallas_call | solution.py:361
  75.1 0.0 all-gather.3.cloned.1.call-update
  75.2 8.6 %all_to_all.5 = f32[4,4,32,128]{3,2,1,0:T(8,128)S(1)} all-to-all(f32[4,4,32,128]{3,2,1,0:T(8,128)S(1)} %bitcast.7), channel_id=1, replica_groups=mesh['dp'=4,'slab'=8] {'dp'}, dimensions={0} | all-to-all | bytes 524288 | tf_op jit(solution)/shard_map/all_to_all | solution.py:376
  83.8 0.0 copy-done.3
  83.8 2.2 %shard_map.132 = f32[128,2048]{1,0:T(8,128)} custom-call(f32[4,128,128]{2,1,0:T(8,128)S(1)} %bitcast.10, bf16[8,64,256]{2,1,0:T(8,128)(2,1)S(1)} %copy-done.3), custom_call_target="tpu_custom_call" | custom-call | tf_op jit(solution)/shard_map/pallas_call | solution.py:379
  86.0 29.1 %all-gather.3.cloned.1.call-done = f32[128,16,128]{2,1,0:T(8,128)} async-done(((f32[16,16,128]{2,1,0:T(8,128)}), f32[128,16,128]{2,1,0:T(8,128)}) %all-gather.3.cloned.1.call-update) | async-done | bytes 1048592 | tf_op jit(solution)/shard_map/all_gather | solution.py:373
  115.2 0.0 copy-done.5
  115.2 0.0 copy-done.6
  115.2 0.0 copy-done.8
  115.2 0.0 copy-done.10
  115.2 0.0 copy-start.1
  115.2 1.2 copy-done.1
  116.4 23.4 %shard_map.134 = bf16[1,16,32,128,128]{4,3,2,1,0:T(8,128)(2,1)} custom-call(f32[2048]{0:T(1024)S(1)} %copy-done.8, f32[2048]{0:T(1024)S(1)} %copy-done.10, bf16[96,256]{1,0:T(8,128)(2,1)S(1)} %copy-done.5, bf16[128,96]{1,0:T(8,128)(2,1)S(1)} %copy-done.6, f32[8,16,16,128]{3,2,1,0:T(8,128)S(1)} %bitcast.9), custom_call_target="tpu_custom_call" | custom-call | tf_op jit(solution)/shard_map/pallas_call | solution.py:387
Async XLA Ops:
  7.2 65.0 %copy-start.2 = (bf16[8,256,64]{2,1,0:T(8,128)(2,1)S(1)}, bf16[8,256,64]{2,1,0:T(8,128)(2,1)}, u32[]{:S(2)}) copy-start(bf16[8,256,64]{2,1,0:T(8,128)(2,1)} %constant.22.clone.e_ref) | copy-start | bytes 786436
  7.2 76.6 %copy-start.3 = (bf16[8,64,256]{2,1,0:T(8,128)(2,1)S(1)}, bf16[8,64,256]{2,1,0:T(8,128)(2,1)}, u32[]{:S(2)}) copy-start(bf16[8,64,256]{2,1,0:T(8,128)(2,1)} %constant.23.clone.e_ref) | copy-start | bytes 786436
  7.2 64.9 %copy-start = (bf16[16,32,2048]{2,1,0:T(8,128)(2,1)S(1)}, bf16[16,32,2048]{2,1,0:T(8,128)(2,1)}, u32[]{:S(2)}) copy-start(bf16[16,32,2048]{2,1,0:T(8,128)(2,1)} %param.15) | copy-start | bytes 6291460
  7.2 108.0 %all-gather.3.cloned.1.call-start = ((), (), s32[]{:S(2)}) async-start(), calls=%async_computation.1 | async-start | bytes 1179648 | tf_op jit(solution)/shard_map/all_gather | solution.py:373
  7.2 1.0 copy-start.4
  8.2 0.7 copy-start.7
  8.9 0.7 copy-start.9
  9.6 0.7 copy-start.11
  10.4 104.8 %copy-start.5 = (bf16[96,256]{1,0:T(8,128)(2,1)S(1)}, bf16[96,256]{1,0:T(8,128)(2,1)}, u32[]{:S(2)}) copy-start(bf16[96,256]{1,0:T(8,128)(2,1)} %constant.20.clone.zi_ref) | copy-start | bytes 147460
  10.4 104.8 %copy-start.6 = (bf16[128,96]{1,0:T(8,128)(2,1)S(1)}, bf16[128,96]{1,0:T(8,128)(2,1)}, u32[]{:S(2)}) copy-start(bf16[128,96]{1,0:T(8,128)(2,1)} %constant.21.clone.yl_ref) | copy-start | bytes 73732
  10.4 104.8 %copy-start.8 = (f32[2048]{0:T(1024)S(1)}, f32[2048]{0:T(1024)}, u32[]{:S(2)}) copy-start(f32[2048]{0:T(1024)} %constant.16.clone.cos_ref) | copy-start | bytes 24580
  10.4 104.8 %copy-start.10 = (f32[2048]{0:T(1024)S(1)}, f32[2048]{0:T(1024)}, u32[]{:S(2)}) copy-start(f32[2048]{0:T(1024)} %constant.17.clone.sin_ref) | copy-start | bytes 24580
  115.2 1.2 copy-start.1
Sparse Core Ops, SparseCore 0:
  75.3 39.8 all-gather.2

commit v3 on v2

--- a/solution.py
+++ b/solution.py
@@ -204,24 +204,115 @@
             lax.fori_loop(1, slabs, sent, 0)
 
 
-def mode_kernel(owned, x_ref, w_ref, e_ref, out_ref):
-    half = owned // 2
-    gr = x_ref[:, 2 * C : 3 * C]
-    gi = x_ref[:, 3 * C : 4 * C]
-    gr = jnp.concatenate([gr] * 4, axis=1)
-    gi = jnp.concatenate([gi] * 4, axis=1)
+def back_products(x_ref, w_ref, e_ref, rows):
+    gr = jnp.concatenate([x_ref[rows, 2 * C : 3 * C]] * 4, axis=1)
+    gi = jnp.concatenate([x_ref[rows, 3 * C : 4 * C]] * 4, axis=1)
     total = None
     width = C * C
     for k in range(width // 128):
-        wr = w_ref[:, k * 128 : (k + 1) * 128].astype(jnp.float32)
-        wi = w_ref[:, width + k * 128 : width + (k + 1) * 128].astype(jnp.float32)
+        wr = w_ref[rows, k * 128 : (k + 1) * 128].astype(jnp.float32)
+        wi = w_ref[rows, width + k * 128 : width + (k + 1) * 128].astype(jnp.float32)
         both = jnp.concatenate([wr * gr + wi * gi, wr * gi - wi * gr], axis=1)
         high, low = split_f32(both)
         part = dot(high, e_ref[k]) + dot(low, e_ref[k])
         total = part if total is None else total + part
-    for a in range(out_ref.shape[0]):
-        mine = total[a * owned : (a + 1) * owned]
-        out_ref[a] = jnp.concatenate([mine[:half], mine[half:]], axis=1)
+    return total
+
+
+def middle_kernel(owned, slabs, dps, cut, x_ref, w_ref, e_ref, wide_ref, out_ref, grad_ref, send, held, swapped, send_sem, recv_sem, dp_send, dp_recv):
+    half = owned // 2
+    me = lax.axis_index("slab")
+    my_dp = lax.axis_index("dp")
+    share = MX // dps * owned
+    part_rows = MX // cut * owned
+
+    def peer(k):
+        return lax.rem(me + k, slabs)
+
+    def dp_peer(k):
+        return lax.rem(my_dp + k, dps)
+
+    def share_of(d):
+        return x_ref.at[pl.ds(pl.multiple_of(d * share, share), share)]
+
+    def gather_copy(at, to, source):
+        return pltpu.make_async_remote_copy(
+            src_ref=send.at[at],
+            dst_ref=held.at[at, source],
+            send_sem=send_sem.at[at, to],
+            recv_sem=recv_sem.at[at, source],
+            device_id=(my_dp, to),
+            device_id_type=pl.DeviceIdType.MESH,
+        )
+
+    def dp_copy(to, source):
+        return pltpu.make_async_remote_copy(
+            src_ref=share_of(to),
+            dst_ref=swapped.at[source],
+            send_sem=dp_send.at[to],
+            recv_sem=dp_recv.at[source],
+            device_id=(to, me),
+            device_id_type=pl.DeviceIdType.MESH,
+        )
+
+    barrier = pltpu.get_barrier_semaphore()
+
+    def greet(k, carry):
+        pl.semaphore_signal(
+            barrier, inc=1, device_id=(my_dp, peer(k)), device_id_type=pl.DeviceIdType.MESH
+        )
+        return carry
+
+    lax.fori_loop(1, slabs, greet, 0)
+    for k in range(1, dps):
+        pl.semaphore_signal(
+            barrier, inc=1, device_id=(dp_peer(k), me), device_id_type=pl.DeviceIdType.MESH
+        )
+
+    for at in range(cut):
+        total = back_products(x_ref, w_ref, e_ref, slice(at * part_rows, (at + 1) * part_rows))
+        for a in range(MX // cut):
+            mine = total[a * owned : (a + 1) * owned]
+            send[at, a] = jnp.concatenate([mine[:half], mine[half:]], axis=1)
+        if at == 0:
+            pl.semaphore_wait(barrier, slabs + dps - 2)
+
+        def push(k, carry):
+            gather_copy(at, peer(k), me).start()
+            return carry
+
+        lax.fori_loop(1, slabs, push, 0)
+        held[at, me] = send[at]
+        if at == 0:
+            for k in range(1, dps):
+                dp_copy(dp_peer(k), my_dp).start()
+            swapped[my_dp] = share_of(my_dp)[...]
+
+    for k in range(1, dps):
+        dp_copy(dp_peer(k), dp_peer(k)).wait_recv()
+    gradient_kernel(swapped, wide_ref, grad_ref)
+
+    for at in range(cut):
+
+        def arrive(k, carry):
+            gather_copy(at, peer(k), peer(k)).wait_recv()
+            return carry
+
+        lax.fori_loop(1, slabs, arrive, 0)
+
+        def place(source, carry):
+            out_ref[source, at * (MX // cut) : (at + 1) * (MX // cut)] = held[at, source]
+            return carry
+
+        lax.fori_loop(0, slabs, place, 0)
+
+        def sent(k, carry):
+            gather_copy(at, peer(k), me).wait_send()
+            return carry
+
+        lax.fori_loop(1, slabs, sent, 0)
+    for k in range(1, dps):
+        dp_copy(dp_peer(k), my_dp).wait_send()
 
 
 def gradient_kernel(x_ref, e_ref, out_ref):
@@ -358,31 +449,30 @@
 
     rows = MX * owned
     cut = 4
-    back = pl.pallas_call(
-        functools.partial(mode_kernel, owned),
-        grid=(cut,),
-        in_specs=[
-            pl.BlockSpec((rows // cut, 4 * C), lambda i: (i, 0)),
-            pl.BlockSpec((rows // cut, 2 * C * C), lambda i: (i, 0)),
-            whole(e_sum),
+    half = owned // 2
+    share = MX // dps
+    spread, grad_weights = pl.pallas_call(
+        functools.partial(middle_kernel, owned, slabs, dps, cut),
+        in_specs=[VMEM] * 4,
+        out_specs=[VMEM] * 2,
+        out_shape=[
+            jax.ShapeDtypeStruct((slabs, MX, half, 4 * C), jnp.float32),
+            jax.ShapeDtypeStruct((share * owned, 2 * C * C), jnp.float32),
         ],
-        out_specs=pl.BlockSpec((MX // cut, owned // 2, 4 * C), lambda i: (i, 0, 0)),
-        out_shape=jax.ShapeDtypeStruct((MX, owned // 2, 4 * C), jnp.float32),
-        compiler_params=params,
-    )(own.reshape(rows, 4 * C), weights.reshape(rows, 2 * C * C), e_sum)
-    spread = lax.all_gather(back, "slab", axis=0, tiled=False)
-
-    share = MX // dps
-    swapped = lax.all_to_all(
-        own.reshape(dps, share, owned, 4 * C), "dp", split_axis=0, concat_axis=0, tiled=True
-    ).reshape(dps, share * owned, 4 * C)
-    grad_weights = pl.pallas_call(
-        gradient_kernel,
-        in_specs=[VMEM, VMEM],
-        out_specs=VMEM,
-        out_shape=jax.ShapeDtypeStruct((share * owned, 2 * C * C), jnp.float32),
-        compiler_params=params,
-    )(swapped, e_wide).reshape(share, owned, 2 * C * C)
+        scratch_shapes=[
+            pltpu.VMEM((cut, MX // cut, half, 4 * C), jnp.float32),
+            pltpu.VMEM((cut, slabs, MX // cut, half, 4 * C), jnp.float32),
+            pltpu.VMEM((dps, share * owned, 4 * C), jnp.float32),
+            pltpu.SemaphoreType.DMA((cut, slabs)),
+            pltpu.SemaphoreType.DMA((cut, slabs)),
+            pltpu.SemaphoreType.DMA((dps,)),
+            pltpu.SemaphoreType.DMA((dps,)),
+        ],
+        compiler_params=pltpu.CompilerParams(
+            vmem_limit_bytes=40 * 2**20, collective_id=1, has_side_effects=True
+        ),
+    )(own.reshape(rows, 4 * C), weights.reshape(rows, 2 * C * C), e_sum, e_wide)
+    grad_weights = grad_weights.reshape(share, owned, 2 * C * C)
 
     grad_field = pl.pallas_call(
         functools.partial(inverse_kernel, planes, group, owned),

time: 147 us -> 117 us (0.80)
  waiting for transfers between devices: 29.1 us -> 0 us
  Pallas kernels: 90.4 us -> 112 us
  between operations: 14.1 us -> 0.71 us
  blocking collectives: 8.63 us -> 0 us
    all_gather x1 -> x0, waiting for transfers between devices: 29.1 us -> none  [body(): spread = lax.all_gather(back, 'slab', axis=0, tiled=False)]
    pallas_call x2 -> x1, Pallas kernels: 5.23 us -> 26.3 us  [body(): pl.pallas_call(functools.partial(middle_kernel, owned, slabs, dps, cut),...]
    all_to_all x1 -> x0, blocking collectives: 8.63 us -> none  [body(): lax.all_to_all(own.reshape(dps, share, owned, 4 * C), 'dp', split_axis=0,...]
    unnamed x24 -> x19, local copies, waits for them, and re-layouts: 4.35 us -> 3.94 us
  transfers between devices with their start and end apart: 1 -> 0, of which waited for: 1 -> 0; matrix products, arithmetic and copies ran while one was open for 0% -> 0% of each run, Pallas kernels for 2% -> 0%
where the time goes in v3:
time: 117 us; the launch traced here: 116 us
  Pallas kernels  112 us (96%)
  local copies, waits for them, and re-layouts  3.94 us (3%)
    pallas_call x1, Pallas kernels, body(): pl.pallas_call(functools.partial(forward_kernel, planes, group, owned, sl...  61.9 us
    pallas_call x1, Pallas kernels, body(): pl.pallas_call(functools.partial(middle_kernel, owned, slabs, dps, cut),...  26.3 us
    pallas_call x1, Pallas kernels, body(): pl.pallas_call(functools.partial(inverse_kernel, planes, group, owned), g...  23.4 us
    unnamed x19, local copies, waits for them, and re-layouts  3.94 us

profile of v3, /device:TPU:0, one launch (start us, length us, event | category | flops | bytes accessed | tf_op | source)
XLA Modules:
  0.0 116.2 jit_solution(14163865279463407816)
XLA Ops:
  0.6 0.0 copy-start.3
  0.6 0.8 copy-done.3
  1.5 0.0 copy-start.6
  1.5 0.7 copy-done.6
  2.2 0.0 copy-start.7
  2.2 0.7 copy-done.7
  2.9 0.0 copy-start.8
  2.9 0.7 copy-done.8
  3.6 0.0 copy-start
  3.6 0.0 copy-start.1
  3.6 0.0 copy-start.2
  3.6 0.0 copy-start.4
  3.6 0.0 copy-start.5
  3.6 61.9 %shard_map.131 = f32[16,32,128]{2,1,0:T(8,128)S(1)} custom-call(f32[2048]{0:T(1024)S(1)} %copy-done.7, f32[2048]{0:T(1024)S(1)} %copy-done.6, bf16[64,128]{1,0:T(8,128)(2,1)S(1)} %copy-done.8, bf16[64,512]{1,0:T(8,128)(2,1)S(1)} %copy-done.3, bf16[1,16,32,128,128]{4,3,2,1,0:T(8,128)(2,1)} %u_ref.1, bf16[1,16,32,128,128]{4,3,2,1,0:T(8,128)(2,1)} %p_ref.1, ...), custom_call_target="tpu_custom_call" | custom-call | tf_op jit(solution)/shard_map/pallas_call | solution.py:432
  65.5 0.0 copy-done
  65.5 0.0 copy-done.1
  65.5 0.0 copy-done.2
  65.5 26.3 %shard_map.132 = (f32[8,16,16,128]{3,2,1,0:T(8,128)S(1)}, f32[128,2048]{1,0:T(8,128)S(1)}) custom-call(f32[512,128]{1,0:T(8,128)S(1)} %bitcast.4, bf16[512,2048]{1,0:T(8,128)(2,1)S(1)} %bitcast.3, bf16[8,256,64]{2,1,0:T(8,128)(2,1)S(1)} %copy-done.1, bf16[8,64,256]{2,1,0:T(8,128)(2,1)S(1)} %copy-done.2), custom_call_target="tpu_custom_call" | custom-call | tf_op jit(solution)/shard_map/pallas_call | solution.py:454
  91.8 0.0 copy-done.4
  91.8 0.0 copy-done.5
  91.8 23.4 %shard_map.133 = bf16[1,16,32,128,128]{4,3,2,1,0:T(8,128)(2,1)} custom-call(f32[2048]{0:T(1024)S(1)} %copy-done.7, f32[2048]{0:T(1024)S(1)} %copy-done.6, bf16[96,256]{1,0:T(8,128)(2,1)S(1)} %copy-done.4, bf16[128,96]{1,0:T(8,128)(2,1)S(1)} %copy-done.5, f32[8,16,16,128]{3,2,1,0:T(8,128)S(1)} %get-tuple-element.5.d_ref), custom_call_target="tpu_custom_call" | custom-call | tf_op jit(solution)/shard_map/pallas_call | solution.py:477
  115.2 1.0 copy.15
Async XLA Ops:
  0.6 0.8 copy-start.3
  1.5 0.7 copy-start.6
  2.2 0.7 copy-start.7
  2.9 0.7 copy-start.8
  3.6 61.9 %copy-start = (bf16[16,32,2048]{2,1,0:T(8,128)(2,1)S(1)}, bf16[16,32,2048]{2,1,0:T(8,128)(2,1)}, u32[]{:S(2)}) copy-start(bf16[16,32,2048]{2,1,0:T(8,128)(2,1)} %param.15) | copy-start | bytes 6291460
  3.6 61.9 %copy-start.1 = (bf16[8,256,64]{2,1,0:T(8,128)(2,1)S(1)}, bf16[8,256,64]{2,1,0:T(8,128)(2,1)}, u32[]{:S(2)}) copy-start(bf16[8,256,64]{2,1,0:T(8,128)(2,1)} %constant.22.clone.e_ref) | copy-start | bytes 786436
  3.6 61.9 %copy-start.2 = (bf16[8,64,256]{2,1,0:T(8,128)(2,1)S(1)}, bf16[8,64,256]{2,1,0:T(8,128)(2,1)}, u32[]{:S(2)}) copy-start(bf16[8,64,256]{2,1,0:T(8,128)(2,1)} %constant.23.clone.wide_ref) | copy-start | bytes 786436
  3.6 88.2 %copy-start.4 = (bf16[96,256]{1,0:T(8,128)(2,1)S(1)}, bf16[96,256]{1,0:T(8,128)(2,1)}, u32[]{:S(2)}) copy-start(bf16[96,256]{1,0:T(8,128)(2,1)} %constant.20.clone.zi_ref) | copy-start | bytes 147460
  3.6 88.2 %copy-start.5 = (bf16[128,96]{1,0:T(8,128)(2,1)S(1)}, bf16[128,96]{1,0:T(8,128)(2,1)}, u32[]{:S(2)}) copy-start(bf16[128,96]{1,0:T(8,128)(2,1)} %constant.21.clone.yl_ref) | copy-start | bytes 73732

commit v4 on v3

--- a/solution.py
+++ b/solution.py
@@ -91,7 +91,7 @@
     return jnp.concatenate([q[1], -q[0], q[3], -q[2]], axis=-1)
 
 
-def forward_kernel(planes, group, owned, slabs, cos_ref, sin_ref, ty_ref, zt_ref, u_ref, p_ref, g_ref, out_ref, rows, send, held, send_sem, recv_sem):
+def forward_kernel(planes, group, owned, slabs, cos_ref, sin_ref, ty_ref, zt_ref, u_ref, p_ref, g_ref, out_ref, rows, send, held, sums, send_sem, recv_sem):
     step = pl.program_id(0)
     steps = planes // group
     me = lax.axis_index("slab")
@@ -163,37 +163,47 @@
     lax.fori_loop(1, slabs, push, 0)
     held[step, me] = send[step, me]
 
+    def absorb(at):
+        def arrive(k, carry):
+            copy(at, peer(k), peer(k)).wait_recv()
+            return carry
+
+        lax.fori_loop(1, slabs, arrive, 0)
+        for low, high in ((0, 5), (5, MX // 2 + 1)):
+
+            def planes_of(src, totals):
+                totals = list(totals)
+                for g in range(group):
+                    value = held[at, src, g]
+                    x = (src * planes + at * group + g) * MX
+                    for n, f in enumerate(range(low, high)):
+                        totals[2 * n] = totals[2 * n] + value * cos_ref[x + f]
+                        if f:
+                            totals[2 * n + 1] = totals[2 * n + 1] + value * sin_ref[x + f]
+                return tuple(totals)
+
+            start = tuple(sums[n] for n in range(2 * low, 2 * high))
+            totals = lax.fori_loop(0, slabs, planes_of, start)
+            for n in range(2 * low, 2 * high):
+                sums[n] = totals[n - 2 * low]
+
+    @pl.when(step == 0)
+    def _():
+        sums[...] = jnp.zeros_like(sums)
+
+    @pl.when(step >= 2)
+    def _():
+        absorb(step - 2)
+
     @pl.when(step == steps - 1)
     def _():
-        for at in range(steps):
-
-            def arrive(k, carry):
-                copy(at, peer(k), peer(k)).wait_recv()
-                return carry
-
-            lax.fori_loop(1, slabs, arrive, 0)
-
-        for low, high in ((0, 5), (5, MX // 2 + 1)):
-
-            def planes_of(src, totals):
-                totals = list(totals)
-                for at in range(steps):
-                    for g in range(group):
-                        value = held[at, src, g]
-                        x = (src * planes + at * group + g) * MX
-                        for n, f in enumerate(range(low, high)):
-                            totals[2 * n] = totals[2 * n] + value * cos_ref[x + f]
-                            if f:
-                                totals[2 * n + 1] = totals[2 * n + 1] + value * sin_ref[x + f]
-                return tuple(totals)
-
-            zero = jnp.zeros((owned, 4 * C), jnp.float32)
-            totals = lax.fori_loop(0, slabs, planes_of, (zero,) * (2 * (high - low)))
-            for n, f in enumerate(range(low, high)):
-                turned = quarter_turn(totals[2 * n + 1])
-                out_ref[f] = totals[2 * n] + turned
-                if 0 < f < MX // 2:
-                    out_ref[MX - f] = totals[2 * n] - turned
+        for at in range(max(steps - 2, 0), steps):
+            absorb(at)
+        for f in range(MX // 2 + 1):
+            turned = quarter_turn(sums[2 * f + 1])
+            out_ref[f] = sums[2 * f] + turned
+            if 0 < f < MX // 2:
+                out_ref[MX - f] = sums[2 * f] - turned
 
         for at in range(steps):
 
@@ -439,6 +449,7 @@
             pltpu.VMEM((4, MY * C, NZ), jnp.float32),
             pltpu.VMEM((steps, slabs, group, owned, 4 * C), jnp.float32),
             pltpu.VMEM((steps, slabs, group, owned, 4 * C), jnp.float32),
+            pltpu.VMEM((MX + 2, owned, 4 * C), jnp.float32),
             pltpu.SemaphoreType.DMA((steps, slabs)),
             pltpu.SemaphoreType.DMA((steps, slabs)),
         ],

time: 117 us -> 115 us (0.983)
  Pallas kernels: 112 us -> 110 us
    pallas_call x1, Pallas kernels: 61.9 us -> 59.8 us  [body(): pl.pallas_call(functools.partial(forward_kernel, planes, group, owned, sl...]
where the time goes in v4:
time: 115 us; the launch traced here: 114 us
  Pallas kernels  110 us (96%)
  local copies, waits for them, and re-layouts  3.94 us (3%)
    pallas_call x1, Pallas kernels, body(): pl.pallas_call(functools.partial(forward_kernel, planes, group, owned, sl...  59.8 us
    pallas_call x1, Pallas kernels, body(): pl.pallas_call(functools.partial(middle_kernel, owned, slabs, dps, cut),...  26.6 us
    pallas_call x1, Pallas kernels, body(): pl.pallas_call(functools.partial(inverse_kernel, planes, group, owned), g...  23.4 us
    unnamed x19, local copies, waits for them, and re-layouts  3.94 us

profile of v4, /device:TPU:0, one launch (start us, length us, event | category | flops | bytes accessed | tf_op | source)
XLA Modules:
  0.0 114.5 jit_solution(3024821510414012266)
XLA Ops:
  0.6 0.0 copy-start.3
  0.6 0.8 copy-done.3
  1.5 0.0 copy-start.6
  1.5 0.7 copy-done.6
  2.2 0.0 copy-start.7
  2.2 0.7 copy-done.7
  2.9 0.0 copy-start.8
  2.9 0.7 copy-done.8
  3.6 0.0 copy-start
  3.6 0.0 copy-start.1
  3.6 0.0 copy-start.2
  3.6 0.0 copy-start.4
  3.6 0.0 copy-start.5
  3.6 59.8 %shard_map.131 = f32[16,32,128]{2,1,0:T(8,128)S(1)} custom-call(f32[2048]{0:T(1024)S(1)} %copy-done.7, f32[2048]{0:T(1024)S(1)} %copy-done.6, bf16[64,128]{1,0:T(8,128)(2,1)S(1)} %copy-done.8, bf16[64,512]{1,0:T(8,128)(2,1)S(1)} %copy-done.3, bf16[1,16,32,128,128]{4,3,2,1,0:T(8,128)(2,1)} %u_ref.1, bf16[1,16,32,128,128]{4,3,2,1,0:T(8,128)(2,1)} %p_ref.1, ...), custom_call_target="tpu_custom_call" | custom-call | tf_op jit(solution)/shard_map/pallas_call | solution.py:442
  63.4 0.0 copy-done
  63.4 0.0 copy-done.1
  63.4 0.0 copy-done.2
  63.4 26.6 %shard_map.132 = (f32[8,16,16,128]{3,2,1,0:T(8,128)S(1)}, f32[128,2048]{1,0:T(8,128)S(1)}) custom-call(f32[512,128]{1,0:T(8,128)S(1)} %bitcast.4, bf16[512,2048]{1,0:T(8,128)(2,1)S(1)} %bitcast.3, bf16[8,256,64]{2,1,0:T(8,128)(2,1)S(1)} %copy-done.1, bf16[8,64,256]{2,1,0:T(8,128)(2,1)S(1)} %copy-done.2), custom_call_target="tpu_custom_call" | custom-call | tf_op jit(solution)/shard_map/pallas_call | solution.py:465
  90.1 0.0 copy-done.4
  90.1 0.0 copy-done.5
  90.1 23.4 %shard_map.133 = bf16[1,16,32,128,128]{4,3,2,1,0:T(8,128)(2,1)} custom-call(f32[2048]{0:T(1024)S(1)} %copy-done.7, f32[2048]{0:T(1024)S(1)} %copy-done.6, bf16[96,256]{1,0:T(8,128)(2,1)S(1)} %copy-done.4, bf16[128,96]{1,0:T(8,128)(2,1)S(1)} %copy-done.5, f32[8,16,16,128]{3,2,1,0:T(8,128)S(1)} %get-tuple-element.5.d_ref), custom_call_target="tpu_custom_call" | custom-call | tf_op jit(solution)/shard_map/pallas_call | solution.py:488
  113.5 1.0 copy.15
Async XLA Ops:
  0.6 0.8 copy-start.3
  1.5 0.7 copy-start.6
  2.2 0.7 copy-start.7
  2.9 0.7 copy-start.8
  3.6 59.8 %copy-start = (bf16[16,32,2048]{2,1,0:T(8,128)(2,1)S(1)}, bf16[16,32,2048]{2,1,0:T(8,128)(2,1)}, u32[]{:S(2)}) copy-start(bf16[16,32,2048]{2,1,0:T(8,128)(2,1)} %param.15) | copy-start | bytes 6291460
  3.6 59.8 %copy-start.1 = (bf16[8,256,64]{2,1,0:T(8,128)(2,1)S(1)}, bf16[8,256,64]{2,1,0:T(8,128)(2,1)}, u32[]{:S(2)}) copy-start(bf16[8,256,64]{2,1,0:T(8,128)(2,1)} %constant.22.clone.e_ref) | copy-start | bytes 786436
  3.6 59.8 %copy-start.2 = (bf16[8,64,256]{2,1,0:T(8,128)(2,1)S(1)}, bf16[8,64,256]{2,1,0:T(8,128)(2,1)}, u32[]{:S(2)}) copy-start(bf16[8,64,256]{2,1,0:T(8,128)(2,1)} %constant.23.clone.wide_ref) | copy-start | bytes 786436
  3.6 86.5 %copy-start.4 = (bf16[96,256]{1,0:T(8,128)(2,1)S(1)}, bf16[96,256]{1,0:T(8,128)(2,1)}, u32[]{:S(2)}) copy-start(bf16[96,256]{1,0:T(8,128)(2,1)} %constant.20.clone.zi_ref) | copy-start | bytes 147460
  3.6 86.5 %copy-start.5 = (bf16[128,96]{1,0:T(8,128)(2,1)S(1)}, bf16[128,96]{1,0:T(8,128)(2,1)}, u32[]{:S(2)}) copy-start(bf16[128,96]{1,0:T(8,128)(2,1)} %constant.21.clone.yl_ref) | copy-start | bytes 73732
